TPU v7x, 1024 devices: a whole 4x4x32 slice. The times are simulated.
1024 devices in a mesh: ctx: 64 (over z_lo, y, core), tp: 16 (over x, z_hi).
Axes of the slice: x: 4, y: 4, z: 32 (z_hi: 4, z_lo: 8; z = z_hi * 8 + z_lo), core: 2. Of those that a mesh axis runs over, the one named last changes fastest.
Arguments:
- queries: bfloat16 [65536, 4096], P('ctx', 'tp'), may hold values from -6 to 6
- keys: bfloat16 [65536, 4096], P('ctx', 'tp'), may hold values from -6 to 6
- values: bfloat16 [65536, 4096], P('ctx', 'tp'), may hold values from -6 to 6
- residues: float32 [16, 4096], P(None, 'tp'), may hold values from -4 to 4
- rates: float32 [16, 4096], P(None, 'tp'), may hold values from 3.8146973e-06 to 0.04
- out_weight: bfloat16 [4096, 4096], P('tp'), may hold values from -0.125 to 0.125
- span_order: int32 [128], replicated, may hold values from 0 to 127, each once
Outputs:
- projected: bfloat16 [65536, 4096], P('ctx', 'tp')
Inputs may be any that keep to these rules, and one draw needn't show every extreme that they name: span_order holds each of 0 .. 127 once.
All inputs are finite; a program needn't handle non-finite values.
Results may differ from a plain program's by a relative error of at most 0.015.
Values may be sent and summed in bfloat16 or wider, within the bound.
A program may use at most 32 MiB of HBM per device.

v0:
```python
import jax
import jax.numpy as jnp
from jax import lax
from jax.sharding import PartitionSpec as P

BLK = 64


def decay_tables(residues, rates, length):
    offsets = jnp.arange(length).astype(jnp.float32)
    scaled = residues * jnp.sqrt(2.0 * rates)
    rising = scaled[:, :, None] * jnp.exp(-rates[:, :, None] * (offsets + 1.0))
    falling = jnp.exp(-rates[:, :, None] * (length - 1.0 - offsets))
    return (scaled, rising, falling)


def local_conv(pieces, residues, rates):
    count, channels, width = pieces.shape
    nblocks = width // BLK
    blocks = pieces.reshape(count, channels, nblocks, BLK)
    scaled, rising, falling = decay_tables(residues, rates, BLK)
    lags = jnp.arange(BLK)
    kernel = jnp.sum(
        scaled[:, :, None] * jnp.exp(-rates[:, :, None] * lags.astype(jnp.float32)), axis=0
    )
    spread = lags[:, None] - lags[None, :]
    toeplitz = jnp.where((spread >= 0)[None], jnp.take(kernel, jnp.maximum(spread, 0), axis=1), 0.0)
    inner = jnp.einsum("cts,ncbs->ncbt", toeplitz, blocks, precision=lax.Precision.HIGHEST)
    block_states = jnp.einsum("ncbs,rcs->nbrc", blocks, falling, precision=lax.Precision.HIGHEST)
    order = jnp.arange(nblocks)
    gaps = order[:, None] - 1 - order[None, :]
    block_decay = jnp.where(
        (gaps >= 0)[:, :, None, None],
        jnp.exp(
            -rates[None, None] * (BLK * jnp.maximum(gaps, 0)).astype(jnp.float32)[:, :, None, None]
        ),
        0.0,
    )
    entering = jnp.einsum(
        "bqrc,nqrc->nbrc", block_decay, block_states, precision=lax.Precision.HIGHEST
    )
    outputs = inner + jnp.einsum(
        "nbrc,rct->ncbt", entering, rising, precision=lax.Precision.HIGHEST
    )
    tail = jnp.exp(-rates[None] * (BLK * (nblocks - 1 - order)).astype(jnp.float32)[:, None, None])
    span_totals = jnp.einsum("brc,nbrc->nrc", tail, block_states, precision=lax.Precision.HIGHEST)
    return (outputs.reshape(count, channels, width), span_totals)


def carry_into(states, targets, residues, rates, width):
    sources = jnp.arange(states.shape[0])
    gaps = targets[:, None] - 1 - sources[None, :]
    decay = jnp.where(
        (gaps >= 0)[:, :, None, None],
        jnp.exp(
            -rates[None, None]
            * (width * jnp.maximum(gaps, 0)).astype(jnp.float32)[:, :, None, None]
        ),
        0.0,
    )
    entering = jnp.einsum("kgrc,grc->krc", decay, states, precision=lax.Precision.HIGHEST)
    scaled, rising, falling = decay_tables(residues, rates, width)
    return jnp.einsum("krc,rct->kct", entering, rising, precision=lax.Precision.HIGHEST)


def local(queries, keys, values, residues, rates, out_weight, span_order):
    tokens, channels = queries.shape
    width = tokens // 2
    total = 2 * lax.axis_size("ctx")
    inverse = jnp.argsort(span_order)
    gated = (keys.astype(jnp.float32) * values.astype(jnp.float32)).astype(jnp.bfloat16)
    grouped = lax.all_to_all(gated.T, "ctx", split_axis=0, concat_axis=1, tiled=True)
    group_size = grouped.shape[0]
    start = lax.axis_index("ctx") * group_size
    group_res = lax.dynamic_slice_in_dim(residues, start, group_size, 1)
    group_rates = lax.dynamic_slice_in_dim(rates, start, group_size, 1)
    pieces = jnp.transpose(grouped.reshape(group_size, total, width), (1, 0, 2))
    ordered = jnp.take(pieces, inverse, axis=0).astype(jnp.float32)
    outputs, states = local_conv(ordered, group_res, group_rates)
    mixed = outputs + carry_into(states, jnp.arange(total), group_res, group_rates, width)
    restored = jnp.take(mixed.astype(jnp.bfloat16), span_order, axis=0)
    flat = jnp.transpose(restored, (1, 0, 2)).reshape(group_size, total * width)
    convolved = lax.all_to_all(flat, "ctx", split_axis=1, concat_axis=0, tiled=True).T
    output = (queries.astype(jnp.float32) * convolved.astype(jnp.float32)).astype(jnp.bfloat16)
    partial_value = jnp.dot(output, out_weight, preferred_element_type=jnp.float32).astype(
        jnp.bfloat16
    )
    summed = lax.psum_scatter(partial_value, "tp", scatter_dimension=1, tiled=True).astype(
        jnp.float32
    )
    return summed.astype(jnp.bfloat16)


def solution(mesh):
    placed = (
        P("ctx", "tp"),
        P("ctx", "tp"),
        P("ctx", "tp"),
        P(None, "tp"),
        P(None, "tp"),
        P("tp", None),
        P(),
    )
    return jax.shard_map(
        local, mesh=mesh, in_specs=placed, out_specs=P("ctx", "tp"), check_vma=False
    )
```

profile of v0, /device:TPU:1, one launch (start us, length us, event | category | flops | bytes accessed | tf_op | source)
XLA Modules:
  0.0 566.5 jit_solution(9433933620524014383)
XLA Ops:
  6.5 0.0 copy-start
  6.5 1.5 fusion.6
  8.0 0.2 copy.76
  8.2 1.0 all_to_all.22
  9.2 18.2 %all-to-all-start = ((bf16[64,4,1024]{2,1,0:T(4,128)(2,1)}), bf16[64,4,1024]{2,1,0:T(4,128)(2,1)S(1)}, u32[]{:S(2)}, u32[]{:S(2)}) async-start(bf16[64,4,1024]{2,1,0:T(4,128)(2,1)} %all_to_all.22), calls=%async_computation | async-start | bytes 1048576 | tf_op jit(solution)/shard_map/all_to_all | solution.py:72
  27.5 0.0 copy-done.1
  27.5 0.0 copy-done.2
  27.5 0.1 constant_dynamic-slice_fusion
  27.6 0.1 copy.100
  27.6 0.1 copy.99
  27.7 0.1 copy.84
  27.8 0.1 multiply_reduce_fusion
  27.9 0.1 copy.82
  28.0 0.1 reshape.215
  28.1 0.1 exponential_bitcast_fusion
  28.2 0.2 copy.94
  28.4 14.1 %gather_fusion = f32[4096,4]{1,0:T(8,128)} fusion(f32[4,64]{0,1:T(8,128)S(1)} %copy.82, s32[4096]{0:T(1024)S(1)} %broadcast_clamp_fusion), kind=kCustom, calls=%fused_computation.2 | custom fusion | bytes 147456 | tf_op jit(solution)/shard_map/jit(_take)/gather | solution.py:27
  42.5 2.3 copy.83
  44.8 0.0 copy-done.3
  44.8 2.5 sort.17
  47.5 0.1 fusion.47
  47.6 0.1 multiply_convert_fusion.2
  47.7 0.1 fusion.26
  47.8 0.1 multiply_convert_fusion.1
  47.8 3.1 exponential_select_fusion
  50.9 6.8 %all-to-all-done = bf16[64,4,1024]{2,1,0:T(4,128)(2,1)S(1)} async-done(((bf16[64,4,1024]{2,1,0:T(4,128)(2,1)}), bf16[64,4,1024]{2,1,0:T(4,128)(2,1)S(1)}, u32[]{:S(2)}, u32[]{:S(2)}) %all-to-all-start) | async-done | bytes 524320 | tf_op jit(solution)/shard_map/all_to_all | solution.py:72
  57.7 1.8 gather_fusion.1
  59.5 1.4 broadcast_select_fusion.1
  60.9 0.4 copy.79
  61.3 0.4 convolution_bitcast_fusion.4
  61.7 0.6 convolution_bitcast_fusion.5
  62.3 0.6 convolution_bitcast_fusion.3
  63.0 1.1 convolution_bitcast_fusion.1
  64.1 10.7 %fusion = f32[16,4,1,128]{3,2,1,0:T(1,128)S(1)} fusion(f32[128,16,4,1]{0,3,2,1:T(1,128)S(1)} %convolution_bitcast_fusion.5, f32[128,128,16,4]{1,2,3,0:T(8,128)} %exponential_select_fusion), kind=kOutput, calls=%fused_computation.4 | convolution fusion | flops 12582912 | bytes 4259840 | tf_op jit(solution)/shard_map/kgrc,grc->krc/dot_general | solution.py:61
  74.8 0.6 fusion.3
  75.4 1.9 fusion.4
  77.3 0.4 copy.88
  77.7 1.0 gather_fusion.2
  78.8 1.1 broadcast_select_fusion
  79.9 6.6 %all-to-all-start.1 = ((bf16[4,64,1024]{2,0,1:T(4,128)(2,1)}), bf16[4,64,1024]{2,0,1:T(4,128)(2,1)S(1)}, u32[]{:S(2)}, u32[]{:S(2)}) async-start(bf16[4,64,1024]{2,0,1:T(4,128)(2,1)} %bitcast.28), calls=%async_computation.1 | async-start | bytes 1048576 | tf_op jit(solution)/shard_map/all_to_all | solution.py:83
  86.5 0.0 reduce-scatter.2.cloned.1.call-start
  86.6 2.1 copy.75
  88.6 28.0 %all-to-all-done.1 = bf16[4,64,1024]{2,0,1:T(4,128)(2,1)S(1)} async-done(((bf16[4,64,1024]{2,0,1:T(4,128)(2,1)}), bf16[4,64,1024]{2,0,1:T(4,128)(2,1)S(1)}, u32[]{:S(2)}, u32[]{:S(2)}) %all-to-all-start.1) | async-done | bytes 524320 | tf_op jit(solution)/shard_map/all_to_all | solution.py:83
  116.7 1.1 convert_bitcast_fusion
  117.8 1.6 reshape.196
  119.4 6.7 %convolution_convert_fusion = bf16[1024,4096]{1,0:T(8,128)(2,1)} fusion(bf16[256,4096]{1,0:T(8,128)(2,1)S(1)} %copy-done, f32[256,1024]{1,0:T(8,128)S(1)} %reshape.196, bf16[1024,256]{0,1:T(8,128)(2,1)} %copy.75), kind=kOutput, calls=%fused_computation.3 | convolution fusion | flops 2152464384 | bytes 12058624 | tf_op jit(solution)/shard_map/dot_general | solution.py:85
  126.1 0.0 reduce-scatter.2.cloned.1.call-update
  126.1 433.5 %reduce-scatter.2.cloned.1.call-done = bf16[1024,256]{1,0:T(8,128)(2,1)} async-done(((bf16[1024,4096]{1,0:T(8,128)(2,1)}), bf16[1024,256]{1,0:T(8,128)(2,1)}) %reduce-scatter.2.cloned.1.call-update) | async-done | bytes 524304 | tf_op jit(solution)/shard_map/reduce_scatter | solution.py:88
  (22 shorter events, 0.1 us)
Async XLA Ops:
  6.5 112.9 %copy-start = (bf16[256,4096]{1,0:T(8,128)(2,1)S(1)}, bf16[256,4096]{1,0:T(8,128)(2,1)}, u32[]{:S(2)}) copy-start(bf16[256,4096]{1,0:T(8,128)(2,1)} %param.14) | copy-start | bytes 6291460
  6.5 20.9 %copy-start.1 = (f32[16,256]{1,0:T(8,128)S(1)}, f32[16,256]{1,0:T(8,128)}, u32[]{:S(2)}) copy-start(f32[16,256]{1,0:T(8,128)} %param.13) | copy-start | bytes 49156
  6.5 20.9 %copy-start.2 = (f32[16,256]{1,0:T(8,128)S(1)}, f32[16,256]{1,0:T(8,128)}, u32[]{:S(2)}) copy-start(f32[16,256]{1,0:T(8,128)} %param.12) | copy-start | bytes 49156
  6.5 38.3 %copy-start.3 = (s32[128]{0:T(128)S(1)}, s32[128]{0:T(128)}, u32[]{:S(2)}) copy-start(s32[128]{0:T(128)} %param.15) | copy-start | bytes 1540
  9.2 48.5 %all-to-all-start = ((bf16[64,4,1024]{2,1,0:T(4,128)(2,1)}), bf16[64,4,1024]{2,1,0:T(4,128)(2,1)S(1)}, u32[]{:S(2)}, u32[]{:S(2)}) async-start(bf16[64,4,1024]{2,1,0:T(4,128)(2,1)} %all_to_all.22), calls=%async_computation | async-start | bytes 1048576 | tf_op jit(solution)/shard_map/all_to_all | solution.py:72
  79.9 36.8 %all-to-all-start.1 = ((bf16[4,64,1024]{2,0,1:T(4,128)(2,1)}), bf16[4,64,1024]{2,0,1:T(4,128)(2,1)S(1)}, u32[]{:S(2)}, u32[]{:S(2)}) async-start(bf16[4,64,1024]{2,0,1:T(4,128)(2,1)} %bitcast.28), calls=%async_computation.1 | async-start | bytes 1048576 | tf_op jit(solution)/shard_map/all_to_all | solution.py:83
  86.5 473.1 %reduce-scatter.2.cloned.1.call-start = ((), (), s32[]{:S(2)}) async-start(), calls=%async_computation.3 | async-start | bytes 8912896 | tf_op jit(solution)/shard_map/reduce_scatter | solution.py:88
Sparse Core Ops, SparseCore 0:
  126.2 433.3 reduce-scatter.1
where the time goes:
time: 568 us; the launch traced here: 566 us
  waiting for transfers between devices  468 us (82%)
  local copies, waits for them, and re-layouts  25.6 us (5%)
  starting transfers between devices  24.9 us (4%)
  matrix products  22.6 us (4%)
  between operations  13.6 us (2%)
  other arithmetic  11.3 us (2%)
    reduce_scatter x1, waiting for transfers between devices, local(): lax.psum_scatter(partial_value, 'tp', scatter_dimension=1, tiled=True)  434 us
    all_to_all x1, waiting for transfers between devices, local(): lax.all_to_all(flat, 'ctx', split_axis=1, concat_axis=0, tiled=True)  28 us
    all_to_all x1, starting transfers between devices, local(): lax.all_to_all(gated.T, 'ctx', split_axis=0, concat_axis=1, tiled=True)  18.2 us
    gather x2, local copies, waits for them, and re-layouts, local_conv(): jnp.take(kernel, jnp.maximum(spread, 0), axis=1)  16.4 us
  transfers between devices with their start and end apart: 3, of which 3 were waited for; matrix products, arithmetic and copies ran while one was open for 4% of the time, Pallas kernels for 0%

commit v1 on v0

v1 whole, which is shorter than its diff:
```python
import jax
import jax.numpy as jnp
from jax import lax
from jax.experimental import pallas as pl
from jax.experimental.pallas import tpu as pltpu
from jax.sharding import PartitionSpec as P

MESH = pl.DeviceIdType.MESH
F32 = jnp.float32
BF16 = jnp.bfloat16

MODES = 16
WIDTH = 256
ROWS = 1024
SPAN = 512
SUB = 64
LANE = 128
CHUNK = 64
STEPS = ROWS // CHUNK
PIECE = WIDTH // 8


def kernel(
    q_hbm, k_hbm, v_hbm, res_ref, rate_ref, w_hbm, order_ref, out_ref,
    q_ref, k_ref, v_ref, w_ref, g_ref, y_ref, inner_ref, state_ref, table_ref,
    sa_ref, cs_ref, cr_ref, enter_ref, o_ref, p_ref, wp_ref, xs_ref, xr_ref, own_ref, zs_ref, zr_ref,
    load_sem, sa_s, sa_r, cb_s, cb_r, w1_s, w1_r, w2_s, w2_r, w3_s, w3_r,
    ag_s, ag_r, x_s, x_r, z_s, z_r,
):
    ctx = lax.axis_index("ctx")
    tp = lax.axis_index("tp")
    z = ctx // 8
    plane = ctx % 8
    x = tp // 4
    h = tp % 4
    pair = h + 1 - 2 * (h % 2)
    other = 3 - h

    def at_plane(to):
        return (z * 8 + to, tp)

    def at_z(to):
        return (to * 8 + plane, tp)

    def at_x(to):
        return (ctx, to * 4 + h)

    at_pair = (ctx, x * 4 + pair)
    at_other = (ctx, x * 4 + other)

    loads = [
        pltpu.make_async_copy(src, dst, load_sem.at[i])
        for i, (src, dst) in enumerate(((k_hbm, k_ref), (v_hbm, v_ref), (w_hbm, w_ref), (q_hbm, q_ref)))
    ]
    for load in loads:
        load.start()

    barrier = pltpu.get_barrier_semaphore()
    partners = [at_plane((plane + i) % 8) for i in range(1, 8)]
    partners += [at_z((z + i) % 8) for i in range(1, 8)]
    partners += [at_x((x + i) % 4) for i in range(1, 4)]
    partners += [at_pair, at_other]
    for partner in partners:
        pl.semaphore_signal(barrier, inc=1, device_id=partner, device_id_type=MESH)

    loads[0].wait()
    loads[1].wait()

    def gate(i, carry):
        rows = pl.ds(pl.multiple_of(i * 64, 64), 64)
        gated = (k_ref[rows].astype(F32) * v_ref[rows].astype(F32)).astype(BF16).astype(F32)
        g_ref[0, rows] = gated[:, :LANE]
        g_ref[1, rows] = gated[:, LANE:]
        return carry

    lax.fori_loop(0, ROWS // 64, gate, 0)

    def wide(row):
        return jnp.broadcast_to(row, (8, LANE))

    sub_index = lax.broadcasted_iota(jnp.int32, (8, LANE), 0)
    sub_float = sub_index.astype(F32)

    for u in range(2):
        lanes = pl.ds(u * LANE, LANE)
        decay = [wide(jnp.exp(-rate_ref[r : r + 1, lanes])) for r in range(MODES)]

        def advance(i, carry, u=u, decay=decay):
            carry = list(carry)
            for j in range(4):
                for s in range(2):
                    new = g_ref[u, pl.ds(s * SPAN + i * 4 + j, 8, stride=SUB), :]
                    for r in range(MODES):
                        carry[s * MODES + r] = carry[s * MODES + r] * decay[r] + new
            return tuple(carry)

        ends = lax.fori_loop(0, SUB // 4, advance, tuple(jnp.zeros((8, LANE), F32) for _ in range(2 * MODES)))
        for r in range(MODES):
            rate = rate_ref[r : r + 1, lanes]
            tail = jnp.exp(-(rate * SUB) * (7.0 - sub_float))
            for s in range(2):
                end = ends[s * MODES + r]
                inner_ref[u, s, r] = end
                state_ref[s, r : r + 1, lanes] = jnp.sum(end * tail, axis=0, keepdims=True)

    sa_ref[plane] = jnp.concatenate([state_ref[0], state_ref[1]], axis=0).astype(BF16)

    pl.semaphore_wait(barrier, len(partners))

    def plane_copy(i):
        return pltpu.make_async_remote_copy(
            src_ref=sa_ref.at[plane], dst_ref=sa_ref.at[plane],
            send_sem=sa_s.at[i - 1], recv_sem=sa_r.at[i - 1],
            device_id=at_plane((plane + i) % 8), device_id_type=MESH,
        )

    for i in range(1, 8):
        plane_copy(i).start()

    loads[2].wait()
    column = ((plane // 2) * 4 + (plane % 2) * (3 - pair) + (1 - plane % 2) * pair) * WIDTH
    rows_z = pl.ds(pl.multiple_of(z * PIECE, PIECE), PIECE)
    w1 = pltpu.make_async_remote_copy(
        src_ref=w_ref.at[rows_z, pl.ds(pl.multiple_of(column, WIDTH), WIDTH)],
        dst_ref=wp_ref.at[plane, rows_z],
        send_sem=w1_s, recv_sem=w1_r, device_id=at_pair, device_id_type=MESH,
    )
    w1.start()

    def w2(i):
        return pltpu.make_async_remote_copy(
            src_ref=wp_ref.at[plane, rows_z], dst_ref=wp_ref.at[plane, rows_z],
            send_sem=w2_s.at[i - 1], recv_sem=w2_r.at[i - 1],
            device_id=at_z((z + i) % 8), device_id_type=MESH,
        )

    def w3(i):
        return pltpu.make_async_remote_copy(
            src_ref=wp_ref.at[plane], dst_ref=wp_ref.at[plane],
            send_sem=w3_s.at[i - 1], recv_sem=w3_r.at[i - 1],
            device_id=at_plane((plane + i) % 8), device_id_type=MESH,
        )

    rate_span = rate_ref[...] * SPAN

    def tables(i, carry):
        for s in range(2):
            target = order_ref[(i * 8 + plane) * 2 + s]
            for j in range(16):
                gap = target - 1 - order_ref[z * 16 + j]
                live = jnp.where(gap >= 0, 1.0, 0.0).astype(F32)
                far = jnp.maximum(gap, 0).astype(F32)
                table_ref[i, s, j] = jnp.exp(rate_span * -far) * live
        return carry

    lax.fori_loop(0, 8, tables, 0)

    for i in range(1, 8):
        plane_copy(i).wait_recv()

    def combine(to):
        sums = []
        for s in range(2):
            total = jnp.zeros((MODES, WIDTH), F32)
            for j in range(16):
                half = pl.ds((j % 2) * MODES, MODES)
                total = total + table_ref[to, s, j] * sa_ref[j // 2, half].astype(F32)
            sums.append(total)
        return sums

    def z_copy(i):
        return pltpu.make_async_remote_copy(
            src_ref=cs_ref.at[i - 1], dst_ref=cr_ref.at[i - 1],
            send_sem=cb_s.at[i - 1], recv_sem=cb_r.at[i - 1],
            device_id=at_z((z + i) % 8), device_id_type=MESH,
        )

    def give(i, carry):
        sums = combine((z + i) % 8)
        cs_ref[i - 1] = jnp.concatenate(sums, axis=0).astype(BF16)
        z_copy(i).start()
        return carry

    lax.fori_loop(1, 8, give, 0)
    for s, total in enumerate(combine(z)):
        enter_ref[s] = total

    w1.wait_recv()
    for i in range(1, 8):
        w2(i).start()

    for u in range(2):
        lanes = pl.ds(u * LANE, LANE)
        decay = [wide(jnp.exp(-rate_ref[r : r + 1, lanes])) for r in range(MODES)]
        scale = [
            wide(res_ref[r : r + 1, lanes] * jnp.sqrt(2.0 * rate_ref[r : r + 1, lanes])) for r in range(MODES)
        ]
        for s in range(2):
            start = []
            for r in range(MODES):
                rate = rate_ref[r : r + 1, lanes]
                run = inner_ref[u, s, r]
                for shift in (1, 2, 4):
                    moved = jnp.where(sub_index >= shift, pltpu.roll(run, shift, 0), 0.0)
                    run = run + moved * jnp.exp(rate * float(-SUB * shift))
                start.append(jnp.where(sub_index >= 1, pltpu.roll(run, 1, 0), 0.0))

            def inside(i, carry, u=u, s=s, decay=decay, scale=scale):
                carry = list(carry)
                for j in range(4):
                    rows = pl.ds(s * SPAN + i * 4 + j, 8, stride=SUB)
                    new = g_ref[u, rows, :]
                    sums = [None] * 4
                    for r in range(MODES):
                        carry[r] = carry[r] * decay[r] + new
                        term = carry[r] * scale[r]
                        sums[r % 4] = term if sums[r % 4] is None else sums[r % 4] + term
                    y_ref[u, rows, :] = (sums[0] + sums[1]) + (sums[2] + sums[3])
                return tuple(carry)

            lax.fori_loop(0, SUB // 4, inside, tuple(start))

    for i in range(1, 8):
        w2(i).wait_recv()
    for i in range(1, 8):
        w3(i).start()

    for i in range(1, 8):
        z_copy(i).wait_recv()

    loads[3].wait()

    def ag(i):
        rows = pl.ds(pl.multiple_of(i * CHUNK, CHUNK), CHUNK)
        return pltpu.make_async_remote_copy(
            src_ref=o_ref.at[rows], dst_ref=p_ref.at[rows],
            send_sem=ag_s.at[i], recv_sem=ag_r.at[i], device_id=at_pair, device_id_type=MESH,
        )

    for s in range(2):
        total = enter_ref[s]
        for i in range(7):
            total = total + cr_ref[i, pl.ds(s * MODES, MODES)].astype(F32)
        total = total * (res_ref[...] * jnp.sqrt(2.0 * rate_ref[...]))
        enter_ref[s] = total
        for u in range(2):
            lanes = pl.ds(u * LANE, LANE)
            decay = []
            start = []
            for r in range(MODES):
                rate = rate_ref[r : r + 1, lanes]
                decay.append(wide(jnp.exp(-rate)))
                start.append(enter_ref[s, r : r + 1, lanes] * jnp.exp(-(rate * SUB) * sub_float))

            def outside(i, carry, u=u, s=s, decay=decay):
                carry = list(carry)
                for j in range(4):
                    rows = pl.ds(s * SPAN + i * 4 + j, 8, stride=SUB)
                    sums = [y_ref[u, rows, :], None, None, None]
                    for r in range(MODES):
                        carry[r] = carry[r] * decay[r]
                        sums[r % 4] = carry[r] if sums[r % 4] is None else sums[r % 4] + carry[r]
                    y_ref[u, rows, :] = (sums[0] + sums[1]) + (sums[2] + sums[3])
                return tuple(carry)

            lax.fori_loop(0, SUB // 4, outside, tuple(start))

        def send(i, carry):
            rows = pl.ds(pl.multiple_of(i * CHUNK, CHUNK), CHUNK)
            for u in range(2):
                lanes = pl.ds(u * LANE, LANE)
                mixed = y_ref[u, rows, :].astype(BF16).astype(F32)
                o_ref[rows, lanes] = (q_ref[rows, lanes].astype(F32) * mixed).astype(BF16)
            ag(i).start()
            return carry

        lax.fori_loop(s * STEPS // 2, (s + 1) * STEPS // 2, send, 0)

    for i in range(1, 8):
        w3(i).wait_recv()

    def x_copy(i, k):
        rows = pl.ds(pl.multiple_of(i * CHUNK, CHUNK), CHUNK)
        return pltpu.make_async_remote_copy(
            src_ref=xs_ref.at[k - 1, rows], dst_ref=xr_ref.at[k - 1, rows],
            send_sem=x_s.at[k - 1, i], recv_sem=x_r.at[k - 1, i],
            device_id=at_x((x + k) % 4), device_id_type=MESH,
        )

    def z_sum(i):
        rows = pl.ds(pl.multiple_of(i * CHUNK, CHUNK), CHUNK)
        return pltpu.make_async_remote_copy(
            src_ref=zs_ref.at[rows], dst_ref=zr_ref.at[rows],
            send_sem=z_s.at[i], recv_sem=z_r.at[i], device_id=at_other, device_id_type=MESH,
        )

    def part(rows, to, side):
        column = (to * 4 + (h if side == 0 else other)) * WIDTH
        mine = jnp.dot(
            o_ref[rows], w_ref[:, pl.ds(pl.multiple_of(column, WIDTH), WIDTH)], preferred_element_type=F32
        )
        theirs = jnp.dot(p_ref[rows], wp_ref[to * 2 + side], preferred_element_type=F32)
        return mine + theirs

    def step(i, carry):
        rows = pl.ds(pl.multiple_of(i * CHUNK, CHUNK), CHUNK)
        ag(i).wait_recv()
        for k in (2, 1, 3):
            to = (x + k) % 4
            for side in range(2):
                xs_ref[k - 1, rows, pl.ds(side * WIDTH, WIDTH)] = part(rows, to, side).astype(BF16)
            x_copy(i, k).start()
        mine = part(rows, x, 1)
        own_ref[rows] = part(rows, x, 0)
        for k in range(1, 4):
            x_copy(i, k).wait_recv()
        for k in range(3):
            mine = mine + xr_ref[k, rows, pl.ds(WIDTH, WIDTH)].astype(F32)
        zs_ref[rows] = mine.astype(BF16)
        z_sum(i).start()
        total = own_ref[rows]
        for k in range(3):
            total = total + xr_ref[k, rows, pl.ds(0, WIDTH)].astype(F32)
        own_ref[rows] = total
        return carry

    lax.fori_loop(0, STEPS, step, 0)

    def finish(i, carry):
        rows = pl.ds(pl.multiple_of(i * CHUNK, CHUNK), CHUNK)
        z_sum(i).wait_recv()
        out_ref[rows] = (own_ref[rows] + zr_ref[rows].astype(F32)).astype(BF16)
        return carry

    lax.fori_loop(0, STEPS, finish, 0)

    for i in range(1, 8):
        plane_copy(i).wait_send()
        z_copy(i).wait_send()
        w2(i).wait_send()
        w3(i).wait_send()
    w1.wait_send()

    def drain(i, carry):
        ag(i).wait_send()
        for k in range(1, 4):
            x_copy(i, k).wait_send()
        z_sum(i).wait_send()
        return carry

    lax.fori_loop(0, STEPS, drain, 0)


def local(queries, keys, values, residues, rates, out_weight, span_order):
    hbm = pl.BlockSpec(memory_space=pl.ANY)
    vmem = pl.BlockSpec(memory_space=pltpu.VMEM)
    smem = pl.BlockSpec(memory_space=pltpu.SMEM)
    dma = pltpu.SemaphoreType.DMA
    return pl.pallas_call(
        kernel,
        out_shape=jax.ShapeDtypeStruct((ROWS, WIDTH), BF16),
        in_specs=[hbm, hbm, hbm, vmem, vmem, hbm, smem],
        out_specs=vmem,
        scratch_shapes=[
            pltpu.VMEM((ROWS, WIDTH), BF16),
            pltpu.VMEM((ROWS, WIDTH), BF16),
            pltpu.VMEM((ROWS, WIDTH), BF16),
            pltpu.VMEM((WIDTH, 16 * WIDTH), BF16),
            pltpu.VMEM((2, ROWS, LANE), F32),
            pltpu.VMEM((2, ROWS, LANE), F32),
            pltpu.VMEM((2, 2, MODES, 8, LANE), F32),
            pltpu.VMEM((2, MODES, WIDTH), F32),
            pltpu.VMEM((8, 2, 16, MODES, WIDTH), F32),
            pltpu.VMEM((8, 2 * MODES, WIDTH), BF16),
            pltpu.VMEM((7, 2 * MODES, WIDTH), BF16),
            pltpu.VMEM((7, 2 * MODES, WIDTH), BF16),
            pltpu.VMEM((2, MODES, WIDTH), F32),
            pltpu.VMEM((ROWS, WIDTH), BF16),
            pltpu.VMEM((ROWS, WIDTH), BF16),
            pltpu.VMEM((8, WIDTH, WIDTH), BF16),
            pltpu.VMEM((3, ROWS, 2 * WIDTH), BF16),
            pltpu.VMEM((3, ROWS, 2 * WIDTH), BF16),
            pltpu.VMEM((ROWS, WIDTH), F32),
            pltpu.VMEM((ROWS, WIDTH), BF16),
            pltpu.VMEM((ROWS, WIDTH), BF16),
            dma((4,)),
            dma((7,)), dma((7,)), dma((7,)), dma((7,)),
            dma, dma,
            dma((7,)), dma((7,)), dma((7,)), dma((7,)),
            dma((STEPS,)), dma((STEPS,)),
            dma((3, STEPS)), dma((3, STEPS)),
            dma((STEPS,)), dma((STEPS,)),
        ],
        compiler_params=pltpu.CompilerParams(
            collective_id=0, has_side_effects=True, vmem_limit_bytes=50 * 2**20
        ),
    )(queries, keys, values, residues, rates, out_weight, span_order)


def solution(mesh):
    placed = (
        P("ctx", "tp"),
        P("ctx", "tp"),
        P("ctx", "tp"),
        P(None, "tp"),
        P(None, "tp"),
        P("tp", None),
        P(),
    )
    return jax.shard_map(
        local, mesh=mesh, in_specs=placed, out_specs=P("ctx", "tp"), check_vma=False
    )
```

time: 568 us -> 225 us (0.40)
  waiting for transfers between devices: 468 us -> 0 us
  Pallas kernels: 0 us -> 218 us
  starting transfers between devices: 24.9 us -> 0 us
  matrix products: 22.6 us -> 0 us
  local copies, waits for them, and re-layouts: 25.6 us -> 6.01 us
  between operations: 13.6 us -> 0.02 us
  other arithmetic: 11.3 us -> 0 us
    reduce_scatter x1 -> x0, waiting for transfers between devices: 434 us -> none  [local(): lax.psum_scatter(partial_value, 'tp', scatter_dimension=1, tiled=True)]
    pallas_call x0 -> x1, Pallas kernels: none -> 218 us  [local(): pl.pallas_call(kernel, out_shape=jax.ShapeDtypeStruct((ROWS, WIDTH), BF16...]
    all_to_all x2 -> x0, waiting for transfers between devices: 34.9 us -> none  [the longest x1 28 us: local(): lax.all_to_all(flat, 'ctx', split_axis=1, concat_axis=0, tiled=True)]
    all_to_all x2 -> x0, starting transfers between devices: 24.8 us -> none  [the longest x1 18.2 us: local(): lax.all_to_all(gated.T, 'ctx', split_axis=0, concat_axis=1, tiled=True)]
    dot_general x8 -> x0, matrix products: 22.6 us -> none  [the longest x1 10.7 us: carry_into(): jnp.einsum('kgrc,grc->krc', decay, states, precision=lax.Precision.HIGHEST)]
    gather x4 -> x0, local copies, waits for them, and re-layouts: 19.3 us -> none  [the longest x2 16.4 us: local_conv(): jnp.take(kernel, jnp.maximum(spread, 0), axis=1)]
  transfers between devices with their start and end apart: 3 -> 0, of which waited for: 3 -> 0; matrix products, arithmetic and copies ran while one was open for 4% -> 0% of each run, Pallas kernels for 0% -> 0%
where the time goes in v1:
time: 225 us; the launch traced here: 224 us
  Pallas kernels  218 us (97%)
  local copies, waits for them, and re-layouts  6.01 us (3%)
    pallas_call x1, Pallas kernels, local(): pl.pallas_call(kernel, out_shape=jax.ShapeDtypeStruct((ROWS, WIDTH), BF16...  218 us
    unnamed x13, local copies, waits for them, and re-layouts  6.01 us

profile of v1, /device:TPU:1, one launch (start us, length us, event | category | flops | bytes accessed | tf_op | source)
XLA Modules:
  0.0 224.3 jit_solution(2479541987278820131)
XLA Ops:
  0.0 0.0 copy-start
  0.0 1.0 copy-done
  1.0 0.0 copy-start.1
  1.0 1.0 copy-done.1
  2.1 0.0 copy-start.2
  2.1 1.0 copy-done.2
  3.1 0.0 copy-start.3
  3.1 0.7 copy-done.3
  3.8 0.0 copy-start.4
  3.8 0.7 copy-done.4
  4.6 0.0 copy-start.5
  4.6 0.7 copy-done.5
  5.2 218.2 %shard_map.73 = bf16[1024,256]{1,0:T(8,128)(2,1)S(1)} custom-call(bf16[1024,256]{1,0:T(8,128)(2,1)S(1)} %copy-done, bf16[1024,256]{1,0:T(8,128)(2,1)S(1)} %copy-done.1, bf16[1024,256]{1,0:T(8,128)(2,1)S(1)} %copy-done.2, f32[16,256]{1,0:T(8,128)S(1)} %copy-done.3, f32[16,256]{1,0:T(8,128)S(1)} %copy-done.4, bf16[256,4096]{1,0:T(8,128)(2,1)} %w_hbm.1, ...), custom_call_target="tpu_custom_call" | custom-call | tf_op jit(solution)/shard_map/pallas_call | solution.py:359
  223.5 0.8 copy.9
Async XLA Ops:
  0.0 1.0 copy-start
  1.0 1.0 copy-start.1
  2.1 1.0 copy-start.2
  3.1 0.7 copy-start.3
  3.8 0.7 copy-start.4
  4.6 0.7 copy-start.5

commit v2 on v1

--- a/solution.py
+++ b/solution.py
@@ -17,14 +17,15 @@
 LANE = 128
 CHUNK = 64
 STEPS = ROWS // CHUNK
+WINDOW = 2
 PIECE = WIDTH // 8
 
 
 def kernel(
-    q_hbm, k_hbm, v_hbm, res_ref, rate_ref, w_hbm, order_ref, out_ref,
-    q_ref, k_ref, v_ref, w_ref, g_ref, y_ref, inner_ref, state_ref, table_ref,
+    q_hbm, k_hbm, v_hbm, res_hbm, rate_hbm, w_hbm, order_hbm, out_ref,
+    q_ref, k_ref, v_ref, w_ref, res_ref, rate_ref, order_ref, g_ref, y_ref, inner_ref, state_ref, table_ref,
     sa_ref, cs_ref, cr_ref, enter_ref, o_ref, p_ref, wp_ref, xs_ref, xr_ref, own_ref, zs_ref, zr_ref,
-    load_sem, sa_s, sa_r, cb_s, cb_r, w1_s, w1_r, w2_s, w2_r, w3_s, w3_r,
+    load_sem, sa_s, sa_r, cb_s, cb_r, w1_s, w1_r, w2_s, w2_r, w3_s, w3_r, w4_s, w4_r,
     ag_s, ag_r, x_s, x_r, z_s, z_r,
 ):
     ctx = lax.axis_index("ctx")
@@ -35,6 +36,7 @@
     h = tp % 4
     pair = h + 1 - 2 * (h % 2)
     other = 3 - h
+    window = WINDOW + jnp.maximum(z - 4, 3 - z)
 
     def at_plane(to):
         return (z * 8 + to, tp)
@@ -50,7 +52,10 @@
 
     loads = [
         pltpu.make_async_copy(src, dst, load_sem.at[i])
-        for i, (src, dst) in enumerate(((k_hbm, k_ref), (v_hbm, v_ref), (w_hbm, w_ref), (q_hbm, q_ref)))
+        for i, (src, dst) in enumerate((
+            (k_hbm, k_ref), (v_hbm, v_ref), (rate_hbm, rate_ref), (res_hbm, res_ref),
+            (order_hbm, order_ref), (q_hbm, q_ref), (w_hbm, w_ref),
+        ))
     ]
     for load in loads:
         load.start()
@@ -81,6 +86,7 @@
     sub_index = lax.broadcasted_iota(jnp.int32, (8, LANE), 0)
     sub_float = sub_index.astype(F32)
 
+    loads[2].wait()
     for u in range(2):
         lanes = pl.ds(u * LANE, LANE)
         decay = [wide(jnp.exp(-rate_ref[r : r + 1, lanes])) for r in range(MODES)]
@@ -117,11 +123,10 @@
     for i in range(1, 8):
         plane_copy(i).start()
 
-    loads[2].wait()
     column = ((plane // 2) * 4 + (plane % 2) * (3 - pair) + (1 - plane % 2) * pair) * WIDTH
     rows_z = pl.ds(pl.multiple_of(z * PIECE, PIECE), PIECE)
     w1 = pltpu.make_async_remote_copy(
-        src_ref=w_ref.at[rows_z, pl.ds(pl.multiple_of(column, WIDTH), WIDTH)],
+        src_ref=w_hbm.at[rows_z, pl.ds(pl.multiple_of(column, WIDTH), WIDTH)],
         dst_ref=wp_ref.at[plane, rows_z],
         send_sem=w1_s, recv_sem=w1_r, device_id=at_pair, device_id_type=MESH,
     )
@@ -134,13 +139,25 @@
             device_id=at_z((z + i) % 8), device_id_type=MESH,
         )
 
+    y = plane // 2
+    core = plane % 2
+
     def w3(i):
         return pltpu.make_async_remote_copy(
             src_ref=wp_ref.at[plane], dst_ref=wp_ref.at[plane],
             send_sem=w3_s.at[i - 1], recv_sem=w3_r.at[i - 1],
-            device_id=at_plane((plane + i) % 8), device_id_type=MESH,
-        )
-
+            device_id=at_plane((y + i) % 4 * 2 + core), device_id_type=MESH,
+        )
+
+    def w4(i):
+        piece = (y + 4 - i) % 4 * 2 + core
+        return pltpu.make_async_remote_copy(
+            src_ref=wp_ref.at[piece], dst_ref=wp_ref.at[piece],
+            send_sem=w4_s.at[i], recv_sem=w4_r.at[i],
+            device_id=at_plane(y * 2 + 1 - core), device_id_type=MESH,
+        )
+
+    loads[4].wait()
     rate_span = rate_ref[...] * SPAN
 
     def tables(i, carry):
@@ -189,6 +206,7 @@
     for i in range(1, 8):
         w2(i).start()
 
+    loads[3].wait()
     for u in range(2):
         lanes = pl.ds(u * LANE, LANE)
         decay = [wide(jnp.exp(-rate_ref[r : r + 1, lanes])) for r in range(MODES)]
@@ -221,14 +239,9 @@
             lax.fori_loop(0, SUB // 4, inside, tuple(start))
 
     for i in range(1, 8):
-        w2(i).wait_recv()
-    for i in range(1, 8):
-        w3(i).start()
-
-    for i in range(1, 8):
         z_copy(i).wait_recv()
 
-    loads[3].wait()
+    loads[5].wait()
 
     def ag(i):
         rows = pl.ds(pl.multiple_of(i * CHUNK, CHUNK), CHUNK)
@@ -265,19 +278,34 @@
 
             lax.fori_loop(0, SUB // 4, outside, tuple(start))
 
-        def send(i, carry):
+        def gated_out(i, carry):
             rows = pl.ds(pl.multiple_of(i * CHUNK, CHUNK), CHUNK)
             for u in range(2):
                 lanes = pl.ds(u * LANE, LANE)
                 mixed = y_ref[u, rows, :].astype(BF16).astype(F32)
                 o_ref[rows, lanes] = (q_ref[rows, lanes].astype(F32) * mixed).astype(BF16)
-            ag(i).start()
             return carry
 
-        lax.fori_loop(s * STEPS // 2, (s + 1) * STEPS // 2, send, 0)
-
-    for i in range(1, 8):
+        lax.fori_loop(s * STEPS // 2, (s + 1) * STEPS // 2, gated_out, 0)
+        if s == 0:
+            for i in range(WINDOW + 3):
+
+                @pl.when(i < window)
+                def _(i=i):
+                    ag(i).start()
+
+    for i in range(1, 8):
+        w2(i).wait_recv()
+    for i in range(1, 4):
+        w3(i).start()
+    w4(0).start()
+
+    for i in range(1, 4):
         w3(i).wait_recv()
+        w4(i).start()
+    for i in range(4):
+        w4(i).wait_recv()
+    loads[6].wait()
 
     def x_copy(i, k):
         rows = pl.ds(pl.multiple_of(i * CHUNK, CHUNK), CHUNK)
@@ -302,34 +330,51 @@
         theirs = jnp.dot(p_ref[rows], wp_ref[to * 2 + side], preferred_element_type=F32)
         return mine + theirs
 
-    def step(i, carry):
-        rows = pl.ds(pl.multiple_of(i * CHUNK, CHUNK), CHUNK)
+    def front(i):
+        rows = pl.ds(pl.multiple_of(i * CHUNK, CHUNK), CHUNK)
+        ag(i).wait_send()
+
+        @pl.when(i + window < STEPS)
+        def _():
+            ag(i + window).start()
+
         ag(i).wait_recv()
         for k in (2, 1, 3):
             to = (x + k) % 4
             for side in range(2):
                 xs_ref[k - 1, rows, pl.ds(side * WIDTH, WIDTH)] = part(rows, to, side).astype(BF16)
             x_copy(i, k).start()
-        mine = part(rows, x, 1)
-        own_ref[rows] = part(rows, x, 0)
+        for side in range(2):
+            own_ref[rows, pl.ds(side * WIDTH, WIDTH)] = part(rows, x, side)
+
+    def back(i):
+        rows = pl.ds(pl.multiple_of(i * CHUNK, CHUNK), CHUNK)
         for k in range(1, 4):
             x_copy(i, k).wait_recv()
-        for k in range(3):
-            mine = mine + xr_ref[k, rows, pl.ds(WIDTH, WIDTH)].astype(F32)
-        zs_ref[rows] = mine.astype(BF16)
-        z_sum(i).start()
-        total = own_ref[rows]
-        for k in range(3):
-            total = total + xr_ref[k, rows, pl.ds(0, WIDTH)].astype(F32)
-        own_ref[rows] = total
-        return carry
-
-    lax.fori_loop(0, STEPS, step, 0)
+        for side in (1, 0):
+            lanes = pl.ds(side * WIDTH, WIDTH)
+            total = own_ref[rows, lanes]
+            for k in range(3):
+                total = total + xr_ref[k, rows, lanes].astype(F32)
+            if side == 1:
+                zs_ref[rows] = total.astype(BF16)
+                z_sum(i).start()
+            else:
+                own_ref[rows, lanes] = total
+
+    def step(i, carry):
+        front(i)
+        back(i - 1)
+        return carry
+
+    front(jnp.int32(0))
+    lax.fori_loop(1, STEPS, step, 0)
+    back(jnp.int32(STEPS - 1))
 
     def finish(i, carry):
         rows = pl.ds(pl.multiple_of(i * CHUNK, CHUNK), CHUNK)
         z_sum(i).wait_recv()
-        out_ref[rows] = (own_ref[rows] + zr_ref[rows].astype(F32)).astype(BF16)
+        out_ref[rows] = (own_ref[rows, pl.ds(0, WIDTH)] + zr_ref[rows].astype(F32)).astype(BF16)
         return carry
 
     lax.fori_loop(0, STEPS, finish, 0)
@@ -338,11 +383,13 @@
         plane_copy(i).wait_send()
         z_copy(i).wait_send()
         w2(i).wait_send()
+    for i in range(1, 4):
         w3(i).wait_send()
+    for i in range(4):
+        w4(i).wait_send()
     w1.wait_send()
 
     def drain(i, carry):
-        ag(i).wait_send()
         for k in range(1, 4):
             x_copy(i, k).wait_send()
         z_sum(i).wait_send()
@@ -354,18 +401,20 @@
 def local(queries, keys, values, residues, rates, out_weight, span_order):
     hbm = pl.BlockSpec(memory_space=pl.ANY)
     vmem = pl.BlockSpec(memory_space=pltpu.VMEM)
-    smem = pl.BlockSpec(memory_space=pltpu.SMEM)
     dma = pltpu.SemaphoreType.DMA
     return pl.pallas_call(
         kernel,
         out_shape=jax.ShapeDtypeStruct((ROWS, WIDTH), BF16),
-        in_specs=[hbm, hbm, hbm, vmem, vmem, hbm, smem],
+        in_specs=[hbm] * 7,
         out_specs=vmem,
         scratch_shapes=[
             pltpu.VMEM((ROWS, WIDTH), BF16),
             pltpu.VMEM((ROWS, WIDTH), BF16),
             pltpu.VMEM((ROWS, WIDTH), BF16),
             pltpu.VMEM((WIDTH, 16 * WIDTH), BF16),
+            pltpu.VMEM((MODES, WIDTH), F32),
+            pltpu.VMEM((MODES, WIDTH), F32),
+            pltpu.SMEM((128,), jnp.int32),
             pltpu.VMEM((2, ROWS, LANE), F32),
             pltpu.VMEM((2, ROWS, LANE), F32),
             pltpu.VMEM((2, 2, MODES, 8, LANE), F32),
@@ -380,19 +429,19 @@
             pltpu.VMEM((8, WIDTH, WIDTH), BF16),
             pltpu.VMEM((3, ROWS, 2 * WIDTH), BF16),
             pltpu.VMEM((3, ROWS, 2 * WIDTH), BF16),
-            pltpu.VMEM((ROWS, WIDTH), F32),
-            pltpu.VMEM((ROWS, WIDTH), BF16),
-            pltpu.VMEM((ROWS, WIDTH), BF16),
-            dma((4,)),
+            pltpu.VMEM((ROWS, 2 * WIDTH), F32),
+            pltpu.VMEM((ROWS, WIDTH), BF16),
+            pltpu.VMEM((ROWS, WIDTH), BF16),
+            dma((7,)),
             dma((7,)), dma((7,)), dma((7,)), dma((7,)),
             dma, dma,
-            dma((7,)), dma((7,)), dma((7,)), dma((7,)),
+            dma((7,)), dma((7,)), dma((3,)), dma((3,)), dma((4,)), dma((4,)),
             dma((STEPS,)), dma((STEPS,)),
             dma((3, STEPS)), dma((3, STEPS)),
             dma((STEPS,)), dma((STEPS,)),
         ],
         compiler_params=pltpu.CompilerParams(
-            collective_id=0, has_side_effects=True, vmem_limit_bytes=50 * 2**20
+            collective_id=0, has_side_effects=True, vmem_limit_bytes=62 * 2**20
         ),
     )(queries, keys, values, residues, rates, out_weight, span_order)
 

time: 225 us -> 164 us (0.73)
  Pallas kernels: 218 us -> 162 us
  local copies, waits for them, and re-layouts: 6.01 us -> 1.87 us
    pallas_call x1, Pallas kernels: 218 us -> 162 us  [local(): pl.pallas_call(kernel, out_shape=jax.ShapeDtypeStruct((ROWS, WIDTH), BF16...]
    unnamed x13 -> x1, local copies, waits for them, and re-layouts: 6.01 us -> 1.87 us
where the time goes in v2:
time: 164 us
  Pallas kernels  162 us (99%)
  local copies, waits for them, and re-layouts  1.87 us (1%)
    pallas_call x1, Pallas kernels, local(): pl.pallas_call(kernel, out_shape=jax.ShapeDtypeStruct((ROWS, WIDTH), BF16...  162 us

profile of v2, /device:TPU:1, one launch (start us, length us, event | category | flops | bytes accessed | tf_op | source)
XLA Modules:
  0.0 164.2 jit_solution(608607567450602223)
XLA Ops:
  0.0 162.3 %shard_map.73 = bf16[1024,256]{1,0:T(8,128)(2,1)} custom-call(bf16[1024,256]{1,0:T(8,128)(2,1)} %q_hbm.1, bf16[1024,256]{1,0:T(8,128)(2,1)} %k_hbm.1, bf16[1024,256]{1,0:T(8,128)(2,1)} %v_hbm.1, f32[16,256]{1,0:T(8,128)} %res_hbm.1, f32[16,256]{1,0:T(8,128)} %rate_hbm.1, bf16[256,4096]{1,0:T(8,128)(2,1)} %w_hbm.1, s32[128]{0:T(128)} %order_hbm.1), custom_call_target="tpu_custom_call" | custom-call | tf_op jit(solution)/shard_map/pallas_call | solution.py:405
  162.3 1.9 %copy.9 = bf16[1024,256]{1,0:T(8,128)(2,1)} copy(bf16[1024,256]{1,0:T(8,128)(2,1)} %shard_map.73) | data formatting | bytes 1048576
